TPU v7x, 512 devices: a whole 4x4x16 slice. The times are simulated.
512 devices in a mesh: lat: 64 (over y, x, z_hi, core), lev: 8 (over z_lo).
Axes of the slice: x: 4, y: 4, z: 16 (z_hi: 2, z_lo: 8; z = z_hi * 8 + z_lo), core: 2. Of those that a mesh axis runs over, the one named last changes fastest.
Arguments:
- spectral: bfloat16 [8, 16, 2, 320, 320], P(None, 'lev', None, 'lat'), may hold values from -0.009765625 to 0.009765625
- legendre: bfloat16 [320, 320, 320], P('lat'), may hold values from -6 to 6
- quad_weight: float32 [320], replicated, may hold values from 1 to 4
- w_in: bfloat16 [128, 256], replicated, may hold values from -0.5 to 0.5
- b_in: float32 [256], replicated, may hold values from -3 to 3
- w_out: bfloat16 [256, 128], replicated, may hold values from -0.375 to 0.375
- b_out: float32 [128], replicated, may hold values from -3 to 3
Outputs:
- tendency_spec: float32 [8, 16, 2, 320, 320], P(None, 'lev', None, 'lat')
All inputs are finite; a program needn't handle non-finite values.
Results may differ from a plain program's by a relative error of at most 0.0055.
Values may be sent and summed in bfloat16 or wider, within the bound.
A program may use at most 64 MiB of HBM per device.

v0:
```python
import math

import jax
import jax.numpy as jnp
from jax import lax
from jax.sharding import PartitionSpec as P

NLON = 1280


def wave_tables(wave_count, lon_count):
    wavenumbers = jnp.arange(wave_count, dtype=jnp.int32)
    longitudes = jnp.arange(lon_count, dtype=jnp.int32)
    phases = wavenumbers[:, None] * longitudes[None, :] % lon_count
    angles = phases.astype(jnp.float32) * (2.0 * math.pi / lon_count)
    cosines = jnp.cos(angles)
    sines = jnp.sin(angles)
    factors = jnp.where(wavenumbers == 0, 1.0, 2.0).astype(jnp.float32)[:, None]
    inverse = jnp.stack([factors * cosines, -factors * sines], axis=1).astype(jnp.bfloat16)
    forward = (jnp.stack([cosines, -sines], axis=1) / lon_count).astype(jnp.bfloat16)
    return (inverse, forward.reshape(2 * wave_count, lon_count))


def shards(spectral, legendre, quad_weight, w_in, b_in, w_out, b_out):
    fields, lev_dev, _, m_dev, degrees = spectral.shape
    channels = fields * lev_dev
    half_lat = legendre.shape[2]
    lat_all = 2 * half_lat
    m_all = m_dev * lax.axis_size("lat")
    lev_count = lax.axis_size("lev")
    levels = lev_dev * lev_count
    features = fields * levels
    lon_count = NLON
    coefficients = spectral.reshape(channels, 2, m_dev, degrees)
    parity = jnp.where(jnp.arange(degrees, dtype=jnp.int32) % 2 == 0, 1.0, -1.0).astype(
        jnp.bfloat16
    )
    full_table = jnp.concatenate([legendre, (legendre * parity[None, :, None])[:, :, ::-1]], axis=2)
    fourier = jnp.einsum(
        "crmn,mnl->mrlc", coefficients, full_table, preferred_element_type=jnp.float32
    ).astype(jnp.bfloat16)
    fourier = fourier.reshape(m_dev, 2, lat_all * channels)
    inverse, forward = wave_tables(m_all, lon_count)
    received = lax.all_to_all(fourier, "lat", split_axis=2, concat_axis=0, tiled=True)
    grid_values = jnp.einsum(
        "mrl,mrx->lx", received, inverse, preferred_element_type=jnp.float32
    ).astype(jnp.bfloat16)
    row_count = grid_values.shape[0]
    lat_dev = row_count // channels
    grid_values = grid_values.reshape(lat_dev * fields, lev_dev, lon_count)
    columns = lax.all_to_all(grid_values, "lev", split_axis=2, concat_axis=1, tiled=True)
    lon_block = columns.shape[2]
    inputs = columns.reshape(lat_dev, features, lon_block)
    hidden = (
        jnp.einsum("ifo,fh->iho", inputs, w_in, preferred_element_type=jnp.float32)
        + b_in[None, :, None]
    )
    hidden = jax.nn.gelu(hidden).astype(jnp.bfloat16)
    tendency = (
        jnp.einsum("iho,hg->igo", hidden, w_out, preferred_element_type=jnp.float32)
        + b_out[None, :, None]
    )
    tendency = tendency.astype(jnp.bfloat16)
    slabs = lax.all_to_all(
        tendency.reshape(lat_dev * fields, levels, lon_block),
        "lev",
        split_axis=1,
        concat_axis=2,
        tiled=True,
    )
    slabs = slabs.reshape(row_count, lon_count)
    row_coeffs = jnp.einsum("kx,lx->kl", forward, slabs, preferred_element_type=jnp.float32).astype(
        jnp.bfloat16
    )
    wave_rows = lax.all_to_all(row_coeffs, "lat", split_axis=0, concat_axis=1, tiled=True)
    wave_rows = wave_rows.reshape(m_dev, 2, lat_all, channels)
    northern = wave_rows[:, :, :half_lat].astype(jnp.float32)
    southern = wave_rows[:, :, half_lat:][:, :, ::-1].astype(jnp.float32)
    weighting = quad_weight[None, None, :, None]
    even_part = ((northern + southern) * weighting).astype(jnp.bfloat16)
    odd_part = ((northern - southern) * weighting).astype(jnp.bfloat16)
    out_even = jnp.einsum(
        "mrjc,mnj->crmn", even_part, legendre[:, 0::2], preferred_element_type=jnp.float32
    )
    out_odd = jnp.einsum(
        "mrjc,mnj->crmn", odd_part, legendre[:, 1::2], preferred_element_type=jnp.float32
    )
    stacked = jnp.stack([out_even, out_odd], axis=-1)
    return stacked.reshape(fields, lev_dev, 2, m_dev, degrees)


def solution(mesh):
    in_specs = (P(None, "lev", None, "lat", None), P("lat", None, None), P(), P(), P(), P(), P())
    out_specs = P(None, "lev", None, "lat", None)
    return jax.shard_map(shards, mesh=mesh, in_specs=in_specs, out_specs=out_specs, check_vma=False)
```

profile of v0, /device:TPU:1, one launch (start us, length us, event | category | flops | bytes accessed | tf_op | source)
XLA Modules:
  0.0 231.8 jit_solution(2167090914626698963)
XLA Ops:
  0.0 1.5 broadcast_multiply_fusion
  1.5 6.3 %reverse = bf16[5,320,384]{2,1,0:T(8,128)(2,1)S(1)} reverse(bf16[5,320,384]{2,1,0:T(8,128)(2,1)S(1)} %bitcast.79), dimensions={2} | reverse | bytes 2457600
  9.7 6.8 %copy.103 = bf16[5,2,640,16]{0,1,3,2:T(2,128)(2,1)} copy(bf16[5,2,640,16]{2,3,1,0:T(8,128)(2,1)S(1)} %fusion.29) | data formatting | bytes 409600 | tf_op jit(solution)/shard_map/reshape | solution.py:42
  16.5 11.9 %reshape.185 = bf16[64,2,800]{2,1,0:T(2,128)(2,1)} reshape(bf16[10240,2,5]{2,1,0:T(2,128)(2,1)} %bitcast.76) | data formatting | bytes 409600
  28.5 22.2 %all-to-all-start = ((bf16[64,2,800]{2,1,0:T(2,128)(2,1)}), bf16[64,2,800]{2,1,0:T(2,128)(2,1)S(1)}, u32[]{:S(2)}, u32[]{:S(2)}) async-start(bf16[64,2,800]{2,1,0:T(2,128)(2,1)} %reshape.185), calls=%async_computation | async-start | bytes 458752 | tf_op jit(solution)/shard_map/all_to_all | solution.py:44
  50.7 7.0 %multiply_convert_fusion = (bf16[320,1,1280]{2,0,1:T(8,128)(2,1)S(1)}, bf16[320,1,1280]{2,0,1:T(8,128)(2,1)S(1)}) fusion(f32[320]{0:T(512)S(1)} %fusion.55, f32[320]{0:T(512)S(1)} %fusion.54), kind=kLoop, calls=%fused_computation.23 | loop fusion | flops 5324800 | bytes 1640960 | tf_op jit(solution)/shard_map/convert.1
  57.7 11.6 %all-to-all-done = bf16[64,2,800]{2,1,0:T(2,128)(2,1)S(1)} async-done(((bf16[64,2,800]{2,1,0:T(2,128)(2,1)}), bf16[64,2,800]{2,1,0:T(2,128)(2,1)S(1)}, u32[]{:S(2)}, u32[]{:S(2)}) %all-to-all-start) | async-done | bytes 204832 | tf_op jit(solution)/shard_map/all_to_all | solution.py:44
  69.3 12.3 %reshape.186 = bf16[10240,2,5]{2,1,0:T(2,128)(2,1)} reshape(bf16[64,2,800]{2,1,0:T(2,128)(2,1)S(1)} %all-to-all-done) | data formatting | bytes 409600
  81.6 11.7 %copy.104 = bf16[5,2,64,160]{3,2,1,0:T(8,128)(2,1)S(1)} copy(bf16[5,2,64,160]{0,1,3,2:T(2,128)(2,1)} %bitcast.77) | data formatting | bytes 409600 | tf_op jit(solution)/shard_map/all_to_all | solution.py:44
  96.1 1.9 copy.86
  98.1 42.6 %all_to_all.64 = bf16[80,2,1280]{0,1,2:T(2,128)(2,1)S(1)} all-to-all(bf16[80,2,1280]{0,1,2:T(2,128)(2,1)S(1)} %copy.86), channel_id=1, replica_groups=mesh['lat'=64,'lev'=8] {'lev'}, dimensions={2} | all-to-all | bytes 819200 | tf_op jit(solution)/shard_map/all_to_all | solution.py:51
  145.2 6.7 %all-to-all-start.2 = ((bf16[80,16,160]{2,0,1:T(8,128)(2,1)}), bf16[80,16,160]{2,0,1:T(8,128)(2,1)}, u32[]{:S(2)}, u32[]{:S(2)}) async-start(bf16[80,16,160]{2,0,1:T(8,128)(2,1)} %copy.91), calls=%async_computation.2 | async-start | bytes 1310720 | tf_op jit(solution)/shard_map/all_to_all | solution.py:64
  151.9 6.6 %fusion.21 = (f32[320,1,1280]{2,0,1:T(8,128)S(1)}, f32[320,1,1280]{2,0,1:T(8,128)S(1)}) fusion(), kind=kLoop, calls=%fused_computation.29 | loop fusion | flops 4096000 | bytes 3276800 | tf_op jit(solution)/shard_map/cos | solution.py:16
  158.9 1.7 copy.79
  160.6 1.6 convert_element_type.84
  162.1 14.0 %all-to-all-done.2 = bf16[80,16,160]{2,0,1:T(8,128)(2,1)} async-done(((bf16[80,16,160]{2,0,1:T(8,128)(2,1)}), bf16[80,16,160]{2,0,1:T(8,128)(2,1)}, u32[]{:S(2)}, u32[]{:S(2)}) %all-to-all-start.2) | async-done | bytes 409632 | tf_op jit(solution)/shard_map/all_to_all | solution.py:64
  178.3 2.1 convolution_convert_fusion
  181.9 15.5 %all-to-all-start.3 = ((bf16[64,2,800]{2,1,0:T(2,128)(2,1)}), bf16[64,2,800]{2,1,0:T(2,128)(2,1)S(1)}, u32[]{:S(2)}, u32[]{:S(2)}) async-start(bf16[64,2,800]{2,1,0:T(2,128)(2,1)} %reshape.187), calls=%async_computation.3 | async-start | bytes 458752 | tf_op jit(solution)/shard_map/all_to_all | solution.py:75
  197.4 3.5 %slice.14 = bf16[5,160,320]{2,1,0:T(8,128)(2,1)} slice(bf16[5,320,320]{2,1,0:T(8,128)(2,1)S(1)} %copy-done.1), slice={[0:5:1], [0:320:2], [0:320:1]} | slice | bytes 1024000 | tf_op jit(solution)/shard_map/slice | solution.py:83
  200.9 3.5 %slice.15 = bf16[5,160,320]{2,1,0:T(8,128)(2,1)} slice(bf16[5,320,320]{2,1,0:T(8,128)(2,1)S(1)} %copy-done.1), slice={[0:5:1], [1:320:2], [0:320:1]} | slice | bytes 1024000 | tf_op jit(solution)/shard_map/slice | solution.py:86
  204.5 11.5 %all-to-all-done.3 = bf16[64,2,800]{2,1,0:T(2,128)(2,1)S(1)} async-done(((bf16[64,2,800]{2,1,0:T(2,128)(2,1)}), bf16[64,2,800]{2,1,0:T(2,128)(2,1)S(1)}, u32[]{:S(2)}, u32[]{:S(2)}) %all-to-all-start.3) | async-done | bytes 204832 | tf_op jit(solution)/shard_map/all_to_all | solution.py:75
  218.8 1.6 copy.108
  221.9 5.6 %copy.97 = f32[16,2,5,160,2]{2,4,3,1,0:T(2,128)} copy(f32[16,2,5,160,2]{3,0,1,2,4:T(8,128)S(1)} %pad_maximum_fusion) | data formatting | bytes 409600 | tf_op jit(solution)/shard_map/stack | solution.py:88
  227.5 4.3 %copy.98 = f32[8,2,2,5,320]{4,2,3,1,0:T(2,128)} copy(f32[8,2,2,5,320]{3,4,2,1,0:T(8,128)} %bitcast.78) | data formatting | bytes 409600 | tf_op jit(solution)/shard_map/reshape | solution.py:89
  (47 shorter events, 17.4 us)
Async XLA Ops:
  0.0 8.4 %copy-start = (bf16[8,2,2,5,320]{4,2,3,1,0:T(2,128)(2,1)S(1)}, bf16[8,2,2,5,320]{4,2,3,1,0:T(2,128)(2,1)}, u32[]{:S(2)}) copy-start(bf16[8,2,2,5,320]{4,2,3,1,0:T(2,128)(2,1)} %param.7) | copy-start | bytes 307204
  7.8 1.3 copy-start.1
  28.5 40.9 %all-to-all-start = ((bf16[64,2,800]{2,1,0:T(2,128)(2,1)}), bf16[64,2,800]{2,1,0:T(2,128)(2,1)S(1)}, u32[]{:S(2)}, u32[]{:S(2)}) async-start(bf16[64,2,800]{2,1,0:T(2,128)(2,1)} %reshape.185), calls=%async_computation | async-start | bytes 458752 | tf_op jit(solution)/shard_map/all_to_all | solution.py:44
  141.5 1.4 copy-start.5
  141.5 1.4 copy-start.6
  141.5 1.3 copy-start.7
  141.5 1.3 copy-start.8
  145.2 30.9 %all-to-all-start.2 = ((bf16[80,16,160]{2,0,1:T(8,128)(2,1)}), bf16[80,16,160]{2,0,1:T(8,128)(2,1)}, u32[]{:S(2)}, u32[]{:S(2)}) async-start(bf16[80,16,160]{2,0,1:T(8,128)(2,1)} %copy.91), calls=%async_computation.2 | async-start | bytes 1310720 | tf_op jit(solution)/shard_map/all_to_all | solution.py:64
  181.9 34.1 %all-to-all-start.3 = ((bf16[64,2,800]{2,1,0:T(2,128)(2,1)}), bf16[64,2,800]{2,1,0:T(2,128)(2,1)S(1)}, u32[]{:S(2)}, u32[]{:S(2)}) async-start(bf16[64,2,800]{2,1,0:T(2,128)(2,1)} %reshape.187), calls=%async_computation.3 | async-start | bytes 458752 | tf_op jit(solution)/shard_map/all_to_all | solution.py:75
  218.8 2.3 copy-start.3
  218.8 2.3 copy-start.4
  218.8 2.7 %copy-start.2 = (bf16[5,160,320]{2,1,0:T(8,128)(2,1)S(1)}, bf16[5,160,320]{2,1,0:T(8,128)(2,1)}, u32[]{:S(2)}) copy-start(bf16[5,160,320]{2,1,0:T(8,128)(2,1)} %slice.15) | copy-start | bytes 1536004
where the time goes:
time: 235 us; the launch traced here: 232 us
  local copies, waits for them, and re-layouts  86 us (37%)
  starting transfers between devices  44.4 us (19%)
  blocking collectives  42.6 us (18%)
  waiting for transfers between devices  37.1 us (16%)
  other arithmetic  15.5 us (7%)
  matrix products  5.85 us (2%)
    all_to_all x1, blocking collectives, shards(): lax.all_to_all(grid_values, 'lev', split_axis=2, concat_axis=1, tiled=True)  42.6 us
    unnamed x27, local copies, waits for them, and re-layouts  35.7 us
    all_to_all x1, starting transfers between devices, shards(): lax.all_to_all(fourier, 'lat', split_axis=2, concat_axis=0, tiled=True)  22.2 us
    all_to_all x1, starting transfers between devices, shards(): lax.all_to_all(row_coeffs, 'lat', split_axis=0, concat_axis=1, tiled=True)  15.5 us
    all_to_all x1, waiting for transfers between devices, shards(): lax.all_to_all(tendency.reshape(lat_dev * fields, levels, lon_block), 'le...  14 us
    all_to_all x2, local copies, waits for them, and re-layouts, shards(): lax.all_to_all(fourier, 'lat', split_axis=2, concat_axis=0, tiled=True)  12 us
    all_to_all x1, waiting for transfers between devices, shards(): lax.all_to_all(fourier, 'lat', split_axis=2, concat_axis=0, tiled=True)  11.6 us
    all_to_all x1, waiting for transfers between devices, shards(): lax.all_to_all(row_coeffs, 'lat', split_axis=0, concat_axis=1, tiled=True)  11.5 us
  transfers between devices with their start and end apart: 3, of which 3 were waited for; matrix products, arithmetic and copies ran while one was open for 10% of the time, Pallas kernels for 0%

commit v1 on v0

v1 whole, which is shorter than its diff:
```python
import functools
import math

import jax
import jax.numpy as jnp
import ml_dtypes
import numpy as np
from jax import lax
from jax.experimental import pallas as pl
from jax.experimental.pallas import tpu as pltpu
from jax.sharding import PartitionSpec as P

MESH = pl.DeviceIdType.MESH
NLON = 1280
WAVES = 320
ZN = 16
PN = 32
SLOTS = 10
OWN_M = 5
KP = 24


def tables():
    m = np.arange(WAVES, dtype=np.int64)
    x = np.arange(NLON, dtype=np.int64)
    angle = ((m[:, None] * x[None, :]) % NLON).astype(np.float32) * np.float32(2.0 * math.pi / NLON)
    cosines, sines = np.cos(angle), np.sin(angle)
    factor = np.where(m == 0, 1.0, 2.0).astype(np.float32)[:, None]
    inverse = np.stack([factor * cosines, -factor * sines], axis=1)
    forward = np.stack([cosines, -sines], axis=1) / np.float32(NLON)

    def arrange(table):
        t = table.reshape(16, 2, 2, OWN_M, 2, NLON).transpose(0, 2, 1, 3, 4, 5).reshape(PN, 4 * OWN_M, NLON)
        padded = np.zeros((PN, KP, NLON), np.float32)
        padded[:, : 4 * OWN_M] = t
        return padded.reshape(PN * KP, NLON).astype(ml_dtypes.bfloat16)

    return np.ascontiguousarray(arrange(inverse).T), arrange(forward)


def device(plane_index, z):
    return {"lat": (plane_index // 2) * 4 + (z // 8) * 2 + plane_index % 2, "lev": z % 8}


def slot_of(z):
    s = (5 * z + 7) // 8
    return s, (8 * s) // 5 == z


def far_first(k):
    return jnp.where(k % 2 == 1, 8 - k // 2, 8 + k // 2)


def kernel(
    spec_ref, leg_hbm, qw_ref, w_in_ref, b_in_ref, w_out_ref, b_out_ref, tinv_hbm, tfwd_hbm,
    out_ref,
    leg, tinv, tfwd, spec32, zsend, zrecv, rows32, psend, precv, tend, bsend, brecv, zbsend, zbrecv,
    load_sem, zs_sem, zr_sem, ps_sem, pr_sem, bs_sem, br_sem, zbs_sem, zbr_sem,
):
    lat = lax.axis_index("lat")
    z = ((lat // 2) % 2) * 8 + lax.axis_index("lev")
    me = (lat // 4) * 2 + lat % 2
    slot, active = slot_of(z)

    leg_load = pltpu.make_async_copy(leg_hbm, leg, load_sem.at[0])
    tinv_load = pltpu.make_async_copy(tinv_hbm, tinv, load_sem.at[1])
    tfwd_load = pltpu.make_async_copy(tfwd_hbm, tfwd, load_sem.at[2])
    leg_load.start()

    barrier = pltpu.get_barrier_semaphore()

    def greet_z(k, carry):
        other = (z + k) % ZN
        _, other_active = slot_of(other)

        @pl.when(jnp.logical_or(active, other_active))
        def _():
            pl.semaphore_signal(barrier, inc=1, device_id=device(me, other), device_id_type=MESH)

        return carry

    lax.fori_loop(1, ZN, greet_z, 0)

    @pl.when(active)
    def _():
        def greet_plane(k, carry):
            pl.semaphore_signal(barrier, inc=1, device_id=device((me + k) % PN, z), device_id_type=MESH)
            return carry

        lax.fori_loop(1, PN, greet_plane, 0)
        tinv_load.start()
        tfwd_load.start()

    for c in range(32):
        values = spec_ref[c].astype(jnp.float32)
        for b, width in enumerate((128, 128, 64)):
            spec32[b, pl.ds(c * 8, OWN_M), 0:width] = values[:, 128 * b : 128 * b + width]
    lane = lax.broadcasted_iota(jnp.int32, (1, WAVES), 1)
    even_lane = lane % 2 == 0
    leg_load.wait()
    for m in range(OWN_M):
        real = jnp.concatenate([spec32[b, pl.ds(m, 16, stride=16), :] for b in range(3)], axis=1)
        imag = jnp.concatenate([spec32[b, pl.ds(8 + m, 16, stride=16), :] for b in range(3)], axis=1)
        both = jnp.concatenate([real, imag], axis=0)[:, :WAVES]
        lhs = jnp.concatenate([jnp.where(even_lane, both, 0.0), jnp.where(even_lane, 0.0, both)], axis=0)
        sums = jnp.dot(lhs.astype(jnp.bfloat16), leg[m], preferred_element_type=jnp.float32)
        north = sums[:32] + sums[32:]
        south = sums[:32] - sums[32:]
        for s in range(SLOTS):
            cols = slice(32 * s, 32 * s + 32)
            piece = jnp.concatenate([north[:16, cols], south[:16, cols], north[16:, cols], south[16:, cols]], axis=1)
            zsend[s, m * 16 : (m + 1) * 16, :] = piece.astype(jnp.bfloat16)

    @pl.when(active)
    def _():
        pl.semaphore_wait(barrier, ZN - 1 + PN - 1)

    @pl.when(jnp.logical_not(active))
    def _():
        pl.semaphore_wait(barrier, SLOTS)

    def send_z(k, carry):
        other = (z + far_first(k)) % ZN
        s, ok = slot_of(other)

        @pl.when(ok)
        def _():
            pltpu.make_async_remote_copy(
                zsend.at[s], zrecv.at[z], zs_sem, zr_sem, device_id=device(me, other), device_id_type=MESH
            ).start()

        return carry

    lax.fori_loop(1, ZN, send_z, 0)

    @pl.when(active)
    def _():
        pltpu.make_async_copy(zsend.at[slot], zrecv.at[z], zr_sem).start()
        pad = jnp.zeros((PN, 128), jnp.float32)
        for hemi in range(2):
            for k in range(20, KP):
                rows32[pl.ds(hemi * KP + k, PN, stride=2 * KP), :] = pad

        row = lax.broadcasted_iota(jnp.int32, (128, 128), 0)
        col = lax.broadcasted_iota(jnp.int32, (128, 128), 1)
        wanted = ((row % 16) // 2) * 16 + (row // 16) * 2 + row % 2
        onehot32 = jnp.where(col == wanted, 1.0, 0.0).astype(jnp.float32)
        onehot = onehot32.astype(jnp.bfloat16)
        eye32 = jnp.where(row == col, 1.0, 0.0).astype(jnp.float32)
        w_in = jnp.dot(onehot, w_in_ref[...], preferred_element_type=jnp.float32).astype(jnp.bfloat16)
        w_out = lax.dot_general(
            w_out_ref[...], onehot, (((1,), (1,)), ((), ())), preferred_element_type=jnp.float32
        ).astype(jnp.bfloat16)
        b_col = jnp.sum(onehot32 * b_out_ref[...], axis=1, keepdims=True)
        b_out = jnp.sum(eye32 * b_col, axis=0, keepdims=True)
        b_in = b_in_ref[...]

        pltpu.make_async_copy(zrecv, zrecv, zr_sem).wait()

        for half in range(2):
            for m in range(OWN_M):
                block = jnp.concatenate(
                    [zrecv[half * 8 + g, m * 16 : (m + 1) * 16, :] for g in range(8)], axis=0
                ).astype(jnp.float32)
                turned = block.T
                for r in range(2):
                    for hemi in range(2):
                        q = (r * 2 + hemi) * 32
                        k = hemi * KP + (half * OWN_M + m) * 2 + r
                        rows32[pl.ds(k, PN, stride=2 * KP), :] = turned[q : q + 32]
        psend[...] = rows32[...].reshape(PN, 2 * KP, 128).astype(jnp.bfloat16)

        def send_plane(k, carry):
            other = (me + k) % PN
            pltpu.make_async_remote_copy(
                psend.at[other], precv.at[me], ps_sem, pr_sem, device_id=device(other, z), device_id_type=MESH
            ).start()
            return carry

        lax.fori_loop(1, PN, send_plane, 0)
        pltpu.make_async_copy(psend.at[me], precv.at[me], pr_sem).start()
        tinv_load.wait()
        tfwd_load.wait()
        pltpu.make_async_copy(precv, precv, pr_sem).wait()

        got = precv[...].astype(jnp.float32)
        waves = jnp.concatenate(
            [got[:, :KP].reshape(PN * KP, 128).astype(jnp.bfloat16), got[:, KP:].reshape(PN * KP, 128).astype(jnp.bfloat16)],
            axis=1,
        )
        tile = 256

        def columns(i, carry):
            rows = pl.ds(pl.multiple_of(i * tile, tile), tile)
            grid = jnp.dot(tinv[rows, :], waves, preferred_element_type=jnp.float32).astype(jnp.bfloat16)
            for hemi in range(2):
                part = slice(hemi * 128, hemi * 128 + 128)
                hidden = jnp.dot(grid[:, part], w_in, preferred_element_type=jnp.float32) + b_in
                hidden = jax.nn.gelu(hidden).astype(jnp.bfloat16)
                value = jnp.dot(hidden, w_out, preferred_element_type=jnp.float32) + b_out
                tend[rows, part] = value.astype(jnp.bfloat16)
            return carry

        lax.fori_loop(0, NLON // tile, columns, 0)
        weight = qw_ref[slot * 32 + me]

        def back(i, carry):
            rows = pl.ds(pl.multiple_of(i * 8 * KP, 8 * KP), 8 * KP)
            coeffs = jnp.dot(tfwd[rows, :], tend[...], preferred_element_type=jnp.float32)
            coeffs = coeffs.astype(jnp.bfloat16).astype(jnp.float32)
            north, south = coeffs[:, :128], coeffs[:, 128:]
            even = ((north + south) * weight).reshape(8, KP, 128)
            odd = ((north - south) * weight).reshape(8, KP, 128)
            bsend[pl.ds(i * 8, 8)] = jnp.concatenate([even, odd], axis=1).astype(jnp.bfloat16)
            return carry

        lax.fori_loop(0, PN // 8, back, 0)

        def return_plane(k, carry):
            other = (me + k) % PN
            pltpu.make_async_remote_copy(
                bsend.at[other], brecv.at[me], bs_sem, br_sem, device_id=device(other, z), device_id_type=MESH
            ).start()
            return carry

        lax.fori_loop(1, PN, return_plane, 0)
        pltpu.make_async_copy(bsend.at[me], brecv.at[me], br_sem).start()
        pltpu.make_async_copy(brecv, brecv, br_sem).wait()

        rows32[...] = brecv[...].astype(jnp.float32).reshape(PN * 2 * KP, 128)
        for half in range(2):
            for m in range(OWN_M):
                blocks = []
                for r in range(2):
                    for par in range(2):
                        k = par * KP + (half * OWN_M + m) * 2 + r
                        blocks.append(rows32[pl.ds(k, PN, stride=2 * KP), :])
                turned = jnp.concatenate(blocks, axis=0).T.astype(jnp.bfloat16)
                for g in range(8):
                    zbsend[half * 8 + g, m * 16 : (m + 1) * 16, :] = turned[g * 16 : (g + 1) * 16]

        def return_z(k, carry):
            other = (z + far_first(k)) % ZN
            pltpu.make_async_remote_copy(
                zbsend.at[other], zbrecv.at[slot], zbs_sem, zbr_sem, device_id=device(me, other), device_id_type=MESH
            ).start()
            return carry

        lax.fori_loop(1, ZN, return_z, 0)
        pltpu.make_async_copy(zbsend.at[z], zbrecv.at[slot], zbr_sem).start()

    pltpu.make_async_copy(zbrecv, zbrecv, zbr_sem).wait()

    for m in range(OWN_M):
        parts = []
        for par in range(2):
            for r in range(2):
                q = (r * 2 + par) * 32
                parts.append(
                    jnp.concatenate(
                        [zbrecv[s, m * 16 : (m + 1) * 16, :].astype(jnp.float32)[:, q : q + 32] for s in range(SLOTS)],
                        axis=1,
                    )
                )
        lhs = jnp.concatenate(parts, axis=0).astype(jnp.bfloat16)
        sums = lax.dot_general(lhs, leg[m], (((1,), (1,)), ((), ())), preferred_element_type=jnp.float32)
        result = jnp.where(even_lane, sums[:32], sums[32:])
        result = jnp.concatenate([result, jnp.zeros((32, 64), jnp.float32)], axis=1)
        for b in range(3):
            cols = slice(128 * b, 128 * b + 128)
            spec32[b, pl.ds(m, 16, stride=16), :] = result[:16, cols]
            spec32[b, pl.ds(8 + m, 16, stride=16), :] = result[16:, cols]
    for c in range(32):
        for b, width in enumerate((128, 128, 64)):
            out_ref[c, :, 128 * b : 128 * b + width] = spec32[b, pl.ds(c * 8, OWN_M), 0:width]

    @pl.when(active)
    def _():
        pltpu.make_async_copy(zsend.at[0:9], zsend.at[0:9], zs_sem).wait()
        pltpu.make_async_copy(psend.at[0:31], psend.at[0:31], ps_sem).wait()
        pltpu.make_async_copy(bsend.at[0:31], bsend.at[0:31], bs_sem).wait()
        pltpu.make_async_copy(zbsend.at[0:15], zbsend.at[0:15], zbs_sem).wait()

    @pl.when(jnp.logical_not(active))
    def _():
        pltpu.make_async_copy(zsend, zsend, zs_sem).wait()


def shards(tinv, tfwd, spectral, legendre, quad_weight, w_in, b_in, w_out, b_out):
    bf16, f32 = jnp.bfloat16, jnp.float32
    vmem, hbm, smem = (pl.BlockSpec(memory_space=s) for s in (pltpu.VMEM, pl.ANY, pltpu.SMEM))
    out = pl.pallas_call(
        kernel,
        out_shape=jax.ShapeDtypeStruct((32, OWN_M, WAVES), f32),
        in_specs=[vmem, hbm, smem, vmem, vmem, vmem, vmem, hbm, hbm],
        out_specs=vmem,
        scratch_shapes=[
            pltpu.VMEM(legendre.shape, bf16),
            pltpu.VMEM((NLON, PN * KP), bf16),
            pltpu.VMEM((PN * KP, NLON), bf16),
            pltpu.VMEM((3, 256, 128), f32),
            pltpu.VMEM((SLOTS, 80, 128), bf16),
            pltpu.VMEM((ZN, 80, 128), bf16),
            pltpu.VMEM((PN * 2 * KP, 128), f32),
            pltpu.VMEM((PN, 2 * KP, 128), bf16),
            pltpu.VMEM((PN, 2 * KP, 128), bf16),
            pltpu.VMEM((NLON, 256), bf16),
            pltpu.VMEM((PN, 2 * KP, 128), bf16),
            pltpu.VMEM((PN, 2 * KP, 128), bf16),
            pltpu.VMEM((ZN, 80, 128), bf16),
            pltpu.VMEM((SLOTS, 80, 128), bf16),
            pltpu.SemaphoreType.DMA((3,)),
        ]
        + [pltpu.SemaphoreType.DMA] * 8,
        compiler_params=pltpu.CompilerParams(collective_id=0, has_side_effects=True, vmem_limit_bytes=48 << 20),
        name="transform_step",
    )(
        spectral.reshape(32, OWN_M, WAVES), legendre, quad_weight,
        w_in, b_in.reshape(1, -1), w_out, b_out.reshape(1, -1), tinv, tfwd,
    )
    return out.reshape(spectral.shape)


def solution(mesh):
    tinv, tfwd = tables()
    in_specs = (P(), P(), P(None, "lev", None, "lat", None), P("lat", None, None), P(), P(), P(), P(), P())
    out_specs = P(None, "lev", None, "lat", None)
    step = jax.shard_map(shards, mesh=mesh, in_specs=in_specs, out_specs=out_specs, check_vma=False)
    return lambda *args: step(jnp.asarray(tinv), jnp.asarray(tfwd), *args)
```

time: 235 us -> 73.7 us (0.31); the launches traced: 232 us -> 73 us
  local copies, waits for them, and re-layouts: 86 us -> 9.81 us
  Pallas kernels: 0 us -> 63.2 us
  starting transfers between devices: 44.4 us -> 0 us
  blocking collectives: 42.6 us -> 0 us
  waiting for transfers between devices: 37.1 us -> 0 us
  other arithmetic: 15.5 us -> 0 us
  matrix products: 5.85 us -> 0 us
    pallas_call x0 -> x1, Pallas kernels: none -> 63.2 us  [shards(): pl.pallas_call(kernel, out_shape=jax.ShapeDtypeStruct((32, OWN_M, WAVES),...]
    all_to_all x3 -> x0, starting transfers between devices: 44.4 us -> none  [the longest x1 22.2 us: shards(): lax.all_to_all(fourier, 'lat', split_axis=2, concat_axis=0, tiled=True)]
    all_to_all x1 -> x0, blocking collectives: 42.6 us -> none  [shards(): lax.all_to_all(grid_values, 'lev', split_axis=2, concat_axis=1, tiled=True)]
    all_to_all x3 -> x0, waiting for transfers between devices: 37.1 us -> none  [the longest x1 14 us: shards(): lax.all_to_all(tendency.reshape(lat_dev * fields, levels, lon_block), 'le...]
    unnamed x27 -> x17, local copies, waits for them, and re-layouts: 35.7 us -> 8.99 us
    reshape x8 -> x1, local copies, waits for them, and re-layouts: 17.8 us -> 0.82 us  [shards(): return out.reshape(spectral.shape)]
    all_to_all x7 -> x0, local copies, waits for them, and re-layouts: 15.1 us -> none  [the longest x2 12 us: shards(): lax.all_to_all(fourier, 'lat', split_axis=2, concat_axis=0, tiled=True)]
    slice x3 -> x0, local copies, waits for them, and re-layouts: 8.09 us -> none  [the longest x1 3.54 us: shards(): legendre[:, 1::2]]
  transfers between devices with their start and end apart: 3 -> 0, of which waited for: 3 -> 0; matrix products, arithmetic and copies ran while one was open for 10% -> 0% of each run, Pallas kernels for 0% -> 0%
where the time goes in v1:
time: 73.7 us; the launch traced here: 73 us
  Pallas kernels  63.2 us (86%)
  local copies, waits for them, and re-layouts  9.81 us (13%)
    pallas_call x1, Pallas kernels, shards(): pl.pallas_call(kernel, out_shape=jax.ShapeDtypeStruct((32, OWN_M, WAVES),...  63.2 us
    unnamed x17, local copies, waits for them, and re-layouts  8.99 us

profile of v1, /device:TPU:1, one launch (start us, length us, event | category | flops | bytes accessed | tf_op | source)
XLA Modules:
  0.0 73.0 jit_solution(18369292599579948206)
XLA Ops:
  0.0 0.9 %copy.10 = bf16[8,2,2,5,320]{4,3,2,1,0:T(8,128)(2,1)S(1)} copy(bf16[8,2,2,5,320]{4,2,3,1,0:T(2,128)(2,1)} %param.9) | data formatting | bytes 204800 | tf_op args[0]
  0.9 0.0 copy-start
  0.9 1.5 %copy-done = bf16[768,1280]{1,0:T(8,128)(2,1)S(1)} copy-done((bf16[768,1280]{1,0:T(8,128)(2,1)S(1)}, bf16[768,1280]{1,0:T(8,128)(2,1)}, u32[]{:S(2)}) %copy-start) | copy-done | bytes 1966104
  2.5 0.0 copy-start.1
  2.5 1.5 %copy-done.1 = bf16[1280,768]{1,0:T(8,128)(2,1)S(1)} copy-done((bf16[1280,768]{1,0:T(8,128)(2,1)S(1)}, bf16[1280,768]{1,0:T(8,128)(2,1)}, u32[]{:S(2)}) %copy-start.1) | copy-done | bytes 1966104
  4.0 0.0 copy-start.2
  4.0 1.3 %copy-done.2 = bf16[5,320,320]{2,1,0:T(8,128)(2,1)S(1)} copy-done((bf16[5,320,320]{2,1,0:T(8,128)(2,1)S(1)}, bf16[5,320,320]{2,1,0:T(8,128)(2,1)}, u32[]{:S(2)}) %copy-start.2) | copy-done | bytes 1024024
  5.3 0.0 copy-start.3
  5.3 0.8 %copy-done.3 = bf16[128,256]{1,0:T(8,128)(2,1)S(1)} copy-done((bf16[128,256]{1,0:T(8,128)(2,1)S(1)}, bf16[128,256]{1,0:T(8,128)(2,1)}, u32[]{:S(2)}) %copy-start.3) | copy-done | bytes 65560
  6.2 0.0 copy-start.4
  6.2 0.8 %copy-done.4 = bf16[256,128]{1,0:T(8,128)(2,1)S(1)} copy-done((bf16[256,128]{1,0:T(8,128)(2,1)S(1)}, bf16[256,128]{1,0:T(8,128)(2,1)}, u32[]{:S(2)}) %copy-start.4) | copy-done | bytes 65560
  7.0 0.0 copy-start.5
  7.0 0.7 copy-done.5
  7.7 0.0 copy-start.6
  7.7 0.7 copy-done.6
  8.4 0.0 copy-start.7
  8.4 0.7 copy-done.7
  9.0 63.2 %transform_step.1 = f32[32,5,320]{2,1,0:T(8,128)S(1)} custom-call(bf16[32,5,320]{2,1,0:T(8,128)(2,1)S(1)} %bitcast.5, bf16[5,320,320]{2,1,0:T(8,128)(2,1)S(1)} %copy-done.2, f32[320]{0:T(512)S(1)} %copy-done.5, bf16[128,256]{1,0:T(8,128)(2,1)S(1)} %copy-done.3, f32[1,256]{1,0:T(1,128)S(1)} %bitcast.6, bf16[256,128]{1,0:T(8,128)(2,1)S(1)} %copy-done.4, ...), custom_call_target="tpu_custom_call" | custom-call | tf_op jit(solution)/shard_map/transform_step/pallas_call | solution.py:292
  72.2 0.8 %copy.11 = f32[8,2,2,5,320]{4,2,3,1,0:T(2,128)} copy(f32[8,2,2,5,320]{4,3,2,1,0:T(8,128)S(1)} %bitcast.4) | data formatting | bytes 409600 | tf_op jit(solution)/shard_map/reshape | solution.py:321
Async XLA Ops:
  0.9 1.5 %copy-start = (bf16[768,1280]{1,0:T(8,128)(2,1)S(1)}, bf16[768,1280]{1,0:T(8,128)(2,1)}, u32[]{:S(2)}) copy-start(bf16[768,1280]{1,0:T(8,128)(2,1)} %constant.5.clone.tfwd_hbm) | copy-start | bytes 5898244
  2.5 1.5 %copy-start.1 = (bf16[1280,768]{1,0:T(8,128)(2,1)S(1)}, bf16[1280,768]{1,0:T(8,128)(2,1)}, u32[]{:S(2)}) copy-start(bf16[1280,768]{1,0:T(8,128)(2,1)} %constant.4.clone.tinv_hbm) | copy-start | bytes 5898244
  4.0 1.3 %copy-start.2 = (bf16[5,320,320]{2,1,0:T(8,128)(2,1)S(1)}, bf16[5,320,320]{2,1,0:T(8,128)(2,1)}, u32[]{:S(2)}) copy-start(bf16[5,320,320]{2,1,0:T(8,128)(2,1)} %leg_hbm.1) | copy-start | bytes 3072004
  5.3 0.8 %copy-start.3 = (bf16[128,256]{1,0:T(8,128)(2,1)S(1)}, bf16[128,256]{1,0:T(8,128)(2,1)}, u32[]{:S(2)}) copy-start(bf16[128,256]{1,0:T(8,128)(2,1)} %w_in_ref.1) | copy-start | bytes 196612
  6.2 0.8 %copy-start.4 = (bf16[256,128]{1,0:T(8,128)(2,1)S(1)}, bf16[256,128]{1,0:T(8,128)(2,1)}, u32[]{:S(2)}) copy-start(bf16[256,128]{1,0:T(8,128)(2,1)} %w_out_ref.1) | copy-start | bytes 196612
  7.0 0.7 copy-start.5
  7.7 0.7 copy-start.6
  8.4 0.7 copy-start.7

commit v2 on v1

v2 whole, which is shorter than its diff:
```python
import functools
import math

import jax
import jax.numpy as jnp
import ml_dtypes
import numpy as np
from jax import lax
from jax.experimental import pallas as pl
from jax.experimental.pallas import tpu as pltpu
from jax.sharding import PartitionSpec as P

MESH = pl.DeviceIdType.MESH
NLON = 1280
WAVES = 320
ZN = 16
PN = 32
SLOTS = 10
OWN_M = 5
TILE = 320
KP = 24


def tables():
    m = np.arange(WAVES, dtype=np.int64)
    x = np.arange(NLON, dtype=np.int64)
    angle = ((m[:, None] * x[None, :]) % NLON).astype(np.float32) * np.float32(2.0 * math.pi / NLON)
    cosines, sines = np.cos(angle), np.sin(angle)
    factor = np.where(m == 0, 1.0, 2.0).astype(np.float32)[:, None]
    inverse = np.stack([factor * cosines, -factor * sines], axis=1)
    forward = np.stack([cosines, -sines], axis=1) / np.float32(NLON)

    def arrange(table):
        t = table.reshape(16, 2, 2, OWN_M, 2, NLON).transpose(0, 2, 1, 3, 4, 5).reshape(PN, 4 * OWN_M, NLON)
        padded = np.zeros((PN, KP, NLON), np.float32)
        padded[:, : 4 * OWN_M] = t
        return padded.reshape(PN * KP, NLON).astype(ml_dtypes.bfloat16)

    return np.ascontiguousarray(arrange(inverse).T), arrange(forward)


def device(plane_index, z):
    return {"lat": (plane_index // 2) * 4 + (z // 8) * 2 + plane_index % 2, "lev": z % 8}


def slot_of(z):
    s = (5 * z + 7) // 8
    return s, (8 * s) // 5 == z


def far_first(k):
    return jnp.where(k % 2 == 1, 8 - k // 2, 8 + k // 2)


def kernel(
    spec_hbm, leg_hbm, qw_hbm, w_in_hbm, b_in_hbm, w_out_hbm, b_out_hbm, tinv_hbm, tfwd_hbm,
    out_ref,
    spec_ref, leg, qw_ref, w_in_ref, b_in_ref, w_out_ref, b_out_ref, tinv, tfwd, spec32, zsend, zrecv, rows32, psend, precv, tend, bsend, brecv, zbsend, zbrecv,
    load_sem, zs_sem, zr_sem, ps_sem, pr_sem, bs_sem, br_sem, zbs_sem, zbr_sem,
):
    lat = lax.axis_index("lat")
    z = ((lat // 2) % 2) * 8 + lax.axis_index("lev")
    me = (lat // 4) * 2 + lat % 2
    slot, active = slot_of(z)

    spec_load = pltpu.make_async_copy(spec_hbm, spec_ref, load_sem.at[0])
    leg_load = pltpu.make_async_copy(leg_hbm, leg, load_sem.at[1])
    weight_load = pltpu.make_async_copy(qw_hbm, qw_ref, load_sem.at[8])
    small_loads = [
        pltpu.make_async_copy(source, target, load_sem.at[2 + i])
        for i, (source, target) in enumerate(
            (
                (w_in_hbm, w_in_ref), (b_in_hbm, b_in_ref), (w_out_hbm, w_out_ref), (b_out_hbm, b_out_ref),
                (tinv_hbm, tinv), (tfwd_hbm, tfwd),
            )
        )
    ]
    spec_load.start()
    leg_load.start()
    weight_load.start()

    barrier = pltpu.get_barrier_semaphore()

    def greet_z(k, carry):
        other = (z + k) % ZN
        _, other_active = slot_of(other)

        @pl.when(jnp.logical_or(active, other_active))
        def _():
            pl.semaphore_signal(barrier, inc=1, device_id=device(me, other), device_id_type=MESH)

        return carry

    lax.fori_loop(1, ZN, greet_z, 0)

    @pl.when(active)
    def _():
        def greet_plane(k, carry):
            pl.semaphore_signal(barrier, inc=1, device_id=device((me + k) % PN, z), device_id_type=MESH)
            return carry

        lax.fori_loop(1, PN, greet_plane, 0)
        for load in small_loads:
            load.start()

    spec_load.wait()
    for i in range(16 * OWN_M):
        values = spec_ref[i].astype(jnp.float32)
        for b, width in enumerate((128, 128, 64)):
            spec32[b, 2 * i : 2 * i + 2, 0:width] = values[:, 128 * b : 128 * b + width]
    lane = lax.broadcasted_iota(jnp.int32, (1, WAVES), 1)
    even_lane = lane % 2 == 0
    leg_load.wait()
    pieces = [[[] for _ in range(SLOTS)] for _ in range(2)]
    for m in range(OWN_M):
        real = jnp.concatenate([spec32[b, pl.ds(2 * m, 16, stride=2 * OWN_M), :] for b in range(3)], axis=1)
        imag = jnp.concatenate([spec32[b, pl.ds(2 * m + 1, 16, stride=2 * OWN_M), :] for b in range(3)], axis=1)
        both = jnp.concatenate([real, imag], axis=0)[:, :WAVES]
        lhs = jnp.concatenate([jnp.where(even_lane, both, 0.0), jnp.where(even_lane, 0.0, both)], axis=0)
        sums = jnp.dot(lhs.astype(jnp.bfloat16), leg[m], preferred_element_type=jnp.float32)
        for h, rows in enumerate((sums[:32] + sums[32:], sums[:32] - sums[32:])):
            for s in range(SLOTS):
                cols = slice(32 * s, 32 * s + 32)
                pieces[h][s].append(jnp.concatenate([rows[8 * i : 8 * i + 8, cols] for i in range(4)], axis=1))
    for h in range(2):
        for s in range(SLOTS):
            zsend[h, s] = jnp.concatenate(pieces[h][s], axis=0).astype(jnp.bfloat16)

    @pl.when(active)
    def _():
        pl.semaphore_wait(barrier, ZN - 1 + PN - 1)

    @pl.when(jnp.logical_not(active))
    def _():
        pl.semaphore_wait(barrier, SLOTS)

    for h in range(2):

        def send_z(k, carry):
            other = (z + far_first(k)) % ZN
            s, ok = slot_of(other)

            @pl.when(ok)
            def _():
                pltpu.make_async_remote_copy(
                    zsend.at[h, s], zrecv.at[h, z], zs_sem.at[h], zr_sem.at[h],
                    device_id=device(me, other), device_id_type=MESH,
                ).start()

            return carry

        lax.fori_loop(1, ZN, send_z, 0)

    @pl.when(active)
    def _():
        for h in range(2):
            pltpu.make_async_copy(zsend.at[h, slot], zrecv.at[h, z], zr_sem.at[h]).start()
        for k in range(20, KP):
            rows32[pl.ds(k, PN, stride=KP), :] = jnp.zeros((PN, 128), jnp.float32)
        for load in small_loads:
            load.wait()

        row = lax.broadcasted_iota(jnp.int32, (128, 128), 0)
        col = lax.broadcasted_iota(jnp.int32, (128, 128), 1)
        wanted = ((row // 64) * 4 + (row % 8) // 2) * 16 + ((row // 8) % 8) * 2 + row % 2
        onehot32 = jnp.where(col == wanted, 1.0, 0.0).astype(jnp.float32)
        onehot = onehot32.astype(jnp.bfloat16)
        eye32 = jnp.where(row == col, 1.0, 0.0).astype(jnp.float32)
        w_in = jnp.dot(onehot, w_in_ref[...], preferred_element_type=jnp.float32).astype(jnp.bfloat16)
        w_out = lax.dot_general(
            w_out_ref[...], onehot, (((1,), (1,)), ((), ())), preferred_element_type=jnp.float32
        ).astype(jnp.bfloat16)
        b_col = jnp.sum(onehot32 * b_out_ref[...], axis=1, keepdims=True)
        b_out = jnp.sum(eye32 * b_col, axis=0, keepdims=True)
        b_in = b_in_ref[...]

        for h in range(2):
            pltpu.make_async_copy(zrecv.at[h], zrecv.at[h], zr_sem.at[h]).wait()
            for half in range(2):
                got = [zrecv[h, half * 8 + g].astype(jnp.float32) for g in range(8)]
                for m in range(OWN_M):
                    turned = jnp.concatenate([t[m * 8 : m * 8 + 8] for t in got], axis=0).T
                    for r in range(2):
                        q = r * 64
                        rows32[pl.ds((half * OWN_M + m) * 2 + r, PN, stride=KP), :] = jnp.concatenate(
                            [turned[q : q + 32], turned[q + 32 : q + 64]], axis=1
                        )
            psend[h] = rows32[...].reshape(PN, KP, 128).astype(jnp.bfloat16)

            def send_plane(k, carry):
                other = (me + k) % PN
                pltpu.make_async_remote_copy(
                    psend.at[h, other], precv.at[h, me], ps_sem.at[h], pr_sem.at[h],
                    device_id=device(other, z), device_id_type=MESH,
                ).start()
                return carry

            lax.fori_loop(1, PN, send_plane, 0)
            pltpu.make_async_copy(psend.at[h, me], precv.at[h, me], pr_sem.at[h]).start()

        for h in range(2):
            pltpu.make_async_copy(precv.at[h], precv.at[h], pr_sem.at[h]).wait()
            waves = precv[h].astype(jnp.float32).reshape(PN * KP, 128).astype(jnp.bfloat16)

            def columns(i, carry):
                rows = pl.ds(pl.multiple_of(i * TILE, TILE), TILE)
                grid = jnp.dot(tinv[rows, :], waves, preferred_element_type=jnp.float32).astype(jnp.bfloat16)
                hidden = jnp.dot(grid, w_in, preferred_element_type=jnp.float32) + b_in
                hidden = jax.nn.gelu(hidden).astype(jnp.bfloat16)
                value = jnp.dot(hidden, w_out, preferred_element_type=jnp.float32) + b_out
                tend[rows, :] = value.astype(jnp.bfloat16)
                return carry

            lax.fori_loop(0, NLON // TILE, columns, 0)
            coeffs = jnp.dot(tfwd[...], tend[...], preferred_element_type=jnp.float32)
            bsend[h] = coeffs.reshape(PN, KP, 128).astype(jnp.bfloat16)

            def return_plane(k, carry):
                other = (me + k) % PN
                pltpu.make_async_remote_copy(
                    bsend.at[h, other], brecv.at[h, me], bs_sem.at[h], br_sem.at[h],
                    device_id=device(other, z), device_id_type=MESH,
                ).start()
                return carry

            lax.fori_loop(1, PN, return_plane, 0)
            pltpu.make_async_copy(bsend.at[h, me], brecv.at[h, me], br_sem.at[h]).start()

        for h in range(2):
            pltpu.make_async_copy(brecv.at[h], brecv.at[h], br_sem.at[h]).wait()
            rows32[...] = brecv[h].astype(jnp.float32).reshape(PN * KP, 128)
            for half in range(2):
                turned = []
                for m in range(OWN_M):
                    blocks = []
                    for r in range(2):
                        block = rows32[pl.ds((half * OWN_M + m) * 2 + r, PN, stride=KP), :]
                        blocks += [block[:, :64], block[:, 64:]]
                    turned.append(jnp.concatenate(blocks, axis=0).T)
                for g in range(8):
                    zbsend[h, half * 8 + g] = jnp.concatenate(
                        [t[g * 8 : g * 8 + 8] for t in turned], axis=0
                    ).astype(jnp.bfloat16)

            def return_z(k, carry):
                other = (z + far_first(k)) % ZN
                pltpu.make_async_remote_copy(
                    zbsend.at[h, other], zbrecv.at[h, slot], zbs_sem.at[h], zbr_sem.at[h],
                    device_id=device(me, other), device_id_type=MESH,
                ).start()
                return carry

            lax.fori_loop(1, ZN, return_z, 0)
            pltpu.make_async_copy(zbsend.at[h, z], zbrecv.at[h, slot], zbr_sem.at[h]).start()

    for h in range(2):
        pltpu.make_async_copy(zbrecv.at[h], zbrecv.at[h], zbr_sem.at[h]).wait()

    weight_load.wait()
    weight = qw_ref[...].reshape(1, WAVES)
    got = [[zbrecv[h, s].astype(jnp.float32) for s in range(SLOTS)] for h in range(2)]
    for m in range(OWN_M):
        north, south = (
            jnp.concatenate(
                [
                    jnp.concatenate(
                        [t[m * 8 : m * 8 + 8, 32 * i : 32 * i + 32] for t in got[h]], axis=1
                    )
                    for i in range(4)
                ],
                axis=0,
            )
            for h in range(2)
        )
        lhs = jnp.concatenate([(north + south) * weight, (north - south) * weight], axis=0).astype(jnp.bfloat16)
        sums = lax.dot_general(lhs, leg[m], (((1,), (1,)), ((), ())), preferred_element_type=jnp.float32)
        result = jnp.where(even_lane, sums[:32], sums[32:])
        result = jnp.concatenate([result, jnp.zeros((32, 64), jnp.float32)], axis=1)
        for b in range(3):
            cols = slice(128 * b, 128 * b + 128)
            spec32[b, pl.ds(2 * m, 16, stride=2 * OWN_M), :] = result[:16, cols]
            spec32[b, pl.ds(2 * m + 1, 16, stride=2 * OWN_M), :] = result[16:, cols]
    for i in range(16 * OWN_M):
        for b, width in enumerate((128, 128, 64)):
            out_ref[i, :, 128 * b : 128 * b + width] = spec32[b, 2 * i : 2 * i + 2, 0:width]

    @pl.when(active)
    def _():
        for h in range(2):
            pltpu.make_async_copy(zsend.at[h, 0:9], zsend.at[h, 0:9], zs_sem.at[h]).wait()
            pltpu.make_async_copy(psend.at[h, 0:31], psend.at[h, 0:31], ps_sem.at[h]).wait()
            pltpu.make_async_copy(bsend.at[h, 0:31], bsend.at[h, 0:31], bs_sem.at[h]).wait()
            pltpu.make_async_copy(zbsend.at[h, 0:15], zbsend.at[h, 0:15], zbs_sem.at[h]).wait()

    @pl.when(jnp.logical_not(active))
    def _():
        for h in range(2):
            pltpu.make_async_copy(zsend.at[h], zsend.at[h], zs_sem.at[h]).wait()


def shards(tinv, tfwd, spectral, legendre, quad_weight, w_in, b_in, w_out, b_out):
    bf16, f32 = jnp.bfloat16, jnp.float32
    vmem, hbm = (pl.BlockSpec(memory_space=s) for s in (pltpu.VMEM, pltpu.HBM))
    out = pl.pallas_call(
        kernel,
        out_shape=jax.ShapeDtypeStruct((16 * OWN_M, 2, WAVES), f32),
        in_specs=[hbm] * 9,
        out_specs=vmem,
        scratch_shapes=[
            pltpu.VMEM((16 * OWN_M, 2, WAVES), bf16),
            pltpu.VMEM(legendre.shape, bf16),
            pltpu.VMEM(quad_weight.shape, f32),
            pltpu.VMEM(w_in.shape, bf16),
            pltpu.VMEM((1, w_in.shape[1]), f32),
            pltpu.VMEM(w_out.shape, bf16),
            pltpu.VMEM((1, w_out.shape[1]), f32),
            pltpu.VMEM((NLON, PN * KP), bf16),
            pltpu.VMEM((PN * KP, NLON), bf16),
            pltpu.VMEM((3, 32 * OWN_M, 128), f32),
            pltpu.VMEM((2, SLOTS, 8 * OWN_M, 128), bf16),
            pltpu.VMEM((2, ZN, 8 * OWN_M, 128), bf16),
            pltpu.VMEM((PN * KP, 128), f32),
            pltpu.VMEM((2, PN, KP, 128), bf16),
            pltpu.VMEM((2, PN, KP, 128), bf16),
            pltpu.VMEM((NLON, 128), bf16),
            pltpu.VMEM((2, PN, KP, 128), bf16),
            pltpu.VMEM((2, PN, KP, 128), bf16),
            pltpu.VMEM((2, ZN, 8 * OWN_M, 128), bf16),
            pltpu.VMEM((2, SLOTS, 8 * OWN_M, 128), bf16),
            pltpu.SemaphoreType.DMA((9,)),
        ]
        + [pltpu.SemaphoreType.DMA((2,))] * 8,
        compiler_params=pltpu.CompilerParams(collective_id=0, has_side_effects=True, vmem_limit_bytes=56 << 20),
        name="transform_step",
    )(
        spectral.transpose(0, 1, 3, 2, 4).reshape(16 * OWN_M, 2, WAVES), legendre, quad_weight,
        w_in, b_in.reshape(1, -1), w_out, b_out.reshape(1, -1), tinv, tfwd,
    )
    return out.reshape(8, 2, OWN_M, 2, WAVES).transpose(0, 1, 3, 2, 4)


def solution(mesh):
    tinv, tfwd = tables()
    in_specs = (P(), P(), P(None, "lev", None, "lat", None), P("lat", None, None), P(), P(), P(), P(), P())
    out_specs = P(None, "lev", None, "lat", None)
    step = jax.shard_map(shards, mesh=mesh, in_specs=in_specs, out_specs=out_specs, check_vma=False)
    return lambda *args: step(jnp.asarray(tinv), jnp.asarray(tfwd), *args)
```

time: 73.7 us -> 61.2 us (0.83)
  local copies, waits for them, and re-layouts: 9.81 us -> 1.69 us
  Pallas kernels: 63.2 us -> 59.3 us
    unnamed x17 -> x1, local copies, waits for them, and re-layouts: 8.99 us -> 1.69 us
    pallas_call x1, Pallas kernels: 63.2 us -> 59.3 us  [shards(): pl.pallas_call(kernel, out_shape=jax.ShapeDtypeStruct((16 * OWN_M, 2, WAV...]
    reshape x1 -> x0, local copies, waits for them, and re-layouts: 0.82 us -> none  [shards(): return out.reshape(spectral.shape)]
where the time goes in v2:
time: 61.2 us; the launch traced here: 61 us
  Pallas kernels  59.3 us (97%)
  local copies, waits for them, and re-layouts  1.69 us (3%)
    pallas_call x1, Pallas kernels, shards(): pl.pallas_call(kernel, out_shape=jax.ShapeDtypeStruct((16 * OWN_M, 2, WAV...  59.3 us
    unnamed x1, local copies, waits for them, and re-layouts  1.69 us

profile of v2, /device:TPU:1, one launch (start us, length us, event | category | flops | bytes accessed | tf_op | source)
XLA Modules:
  0.0 61.0 jit_solution(16153910061476580494)
XLA Ops:
  0.0 59.3 %transform_step.1 = f32[80,2,320]{2,1,0:T(2,128)} custom-call(bf16[80,2,320]{2,1,0:T(2,128)(2,1)} %bitcast.9, bf16[5,320,320]{2,1,0:T(8,128)(2,1)} %leg_hbm.1, f32[320]{0:T(512)} %qw_hbm.1, bf16[128,256]{1,0:T(8,128)(2,1)} %w_in_hbm.1, f32[1,256]{1,0:T(1,128)} %bitcast.10, bf16[256,128]{1,0:T(8,128)(2,1)} %w_out_hbm.1, f32[1,128]{1,0:T(1,128)} %bitcast.11, ...), custom_call_target="tpu_custom_call" | custom-call | tf_op jit(solution)/shard_map/transform_step/pallas_call | solution.py:304
  59.3 1.7 %copy.11 = f32[8,2,2,5,320]{4,2,3,1,0:T(2,128)} copy(f32[8,2,2,5,320]{4,2,3,1,0:T(2,128)} %bitcast.8) | data formatting | bytes 409600

commit v3 on v2

--- a/solution.py
+++ b/solution.py
@@ -17,7 +17,6 @@
 PN = 32
 SLOTS = 10
 OWN_M = 5
-TILE = 320
 KP = 24
 
 
@@ -48,14 +47,29 @@
     return s, (8 * s) // 5 == z
 
 
-def far_first(k):
-    return jnp.where(k % 2 == 1, 8 - k // 2, 8 + k // 2)
+FAR_FIRST = (8, 7, 9, 6, 10, 5, 11, 4, 12, 3, 13, 2, 14, 1, 15)
+RETURN_ORDER = (((0, 0, 6),), ((1, 0, 3), (1, 3, 6), (0, 6, 16), (1, 6, 16)))
+
+
+def away(step):
+    return min(step, 4 - step)
+
+
+PLANE_FAR_FIRST = sorted(
+    [(dy, dx, dc) for dy in range(4) for dx in range(4) for dc in range(2) if dy or dx or dc],
+    key=lambda step: -(away(step[0]) + away(step[1])),
+)
+
+
+def plane_other(me, step):
+    y, x, core = me // 8, (me // 2) % 4, me % 2
+    return (((y + step[0]) % 4) * 4 + (x + step[1]) % 4) * 2 + (core + step[2]) % 2
 
 
 def kernel(
-    spec_hbm, leg_hbm, qw_hbm, w_in_hbm, b_in_hbm, w_out_hbm, b_out_hbm, tinv_hbm, tfwd_hbm,
-    out_ref,
-    spec_ref, leg, qw_ref, w_in_ref, b_in_ref, w_out_ref, b_out_ref, tinv, tfwd, spec32, zsend, zrecv, rows32, psend, precv, tend, bsend, brecv, zbsend, zbrecv,
+    spec_hbm, leg_hbm, w_in_hbm, b_in_hbm, w_out_hbm, b_out_hbm, tinv_hbm, tfwd_hbm,
+    zbrecv,
+    spec_ref, leg, w_in_ref, b_in_ref, w_out_ref, b_out_ref, tinv, tfwd, spec32, zsend, zrecv, rows32, psend, precv, tend, bsend, brecv, zbsend,
     load_sem, zs_sem, zr_sem, ps_sem, pr_sem, bs_sem, br_sem, zbs_sem, zbr_sem,
 ):
     lat = lax.axis_index("lat")
@@ -65,7 +79,6 @@
 
     spec_load = pltpu.make_async_copy(spec_hbm, spec_ref, load_sem.at[0])
     leg_load = pltpu.make_async_copy(leg_hbm, leg, load_sem.at[1])
-    weight_load = pltpu.make_async_copy(qw_hbm, qw_ref, load_sem.at[8])
     small_loads = [
         pltpu.make_async_copy(source, target, load_sem.at[2 + i])
         for i, (source, target) in enumerate(
@@ -77,11 +90,10 @@
     ]
     spec_load.start()
     leg_load.start()
-    weight_load.start()
 
     barrier = pltpu.get_barrier_semaphore()
 
-    def greet_z(k, carry):
+    for k in FAR_FIRST:
         other = (z + k) % ZN
         _, other_active = slot_of(other)
 
@@ -89,17 +101,11 @@
         def _():
             pl.semaphore_signal(barrier, inc=1, device_id=device(me, other), device_id_type=MESH)
 
-        return carry
-
-    lax.fori_loop(1, ZN, greet_z, 0)
-
     @pl.when(active)
     def _():
-        def greet_plane(k, carry):
-            pl.semaphore_signal(barrier, inc=1, device_id=device((me + k) % PN, z), device_id_type=MESH)
-            return carry
-
-        lax.fori_loop(1, PN, greet_plane, 0)
+        for step in PLANE_FAR_FIRST:
+            other = plane_other(me, step)
+            pl.semaphore_signal(barrier, inc=1, device_id=device(other, z), device_id_type=MESH)
         for load in small_loads:
             load.start()
 
@@ -134,22 +140,29 @@
     def _():
         pl.semaphore_wait(barrier, SLOTS)
 
+    def wait_z(h):
+        @pl.when(active)
+        def _():
+            pltpu.make_async_copy(zsend.at[h, 0:9], zsend.at[h, 0:9], zs_sem.at[h]).wait()
+
+        @pl.when(jnp.logical_not(active))
+        def _():
+            pltpu.make_async_copy(zsend.at[h], zsend.at[h], zs_sem.at[h]).wait()
+
     for h in range(2):
-
-        def send_z(k, carry):
-            other = (z + far_first(k)) % ZN
-            s, ok = slot_of(other)
-
-            @pl.when(ok)
+        for k in FAR_FIRST:
+            other = (z + k) % ZN
+            other_slot, other_active = slot_of(other)
+
+            @pl.when(other_active)
             def _():
                 pltpu.make_async_remote_copy(
-                    zsend.at[h, s], zrecv.at[h, z], zs_sem.at[h], zr_sem.at[h],
+                    zsend.at[h, other_slot], zrecv.at[h, z], zs_sem.at[h], zr_sem.at[h],
                     device_id=device(me, other), device_id_type=MESH,
                 ).start()
 
-            return carry
-
-        lax.fori_loop(1, ZN, send_z, 0)
+        if h == 0:
+            wait_z(0)
 
     @pl.when(active)
     def _():
@@ -187,44 +200,44 @@
                         )
             psend[h] = rows32[...].reshape(PN, KP, 128).astype(jnp.bfloat16)
 
-            def send_plane(k, carry):
-                other = (me + k) % PN
+            for step in PLANE_FAR_FIRST:
+                other = plane_other(me, step)
                 pltpu.make_async_remote_copy(
                     psend.at[h, other], precv.at[h, me], ps_sem.at[h], pr_sem.at[h],
                     device_id=device(other, z), device_id_type=MESH,
                 ).start()
-                return carry
-
-            lax.fori_loop(1, PN, send_plane, 0)
             pltpu.make_async_copy(psend.at[h, me], precv.at[h, me], pr_sem.at[h]).start()
 
         for h in range(2):
             pltpu.make_async_copy(precv.at[h], precv.at[h], pr_sem.at[h]).wait()
             waves = precv[h].astype(jnp.float32).reshape(PN * KP, 128).astype(jnp.bfloat16)
 
-            def columns(i, carry):
-                rows = pl.ds(pl.multiple_of(i * TILE, TILE), TILE)
-                grid = jnp.dot(tinv[rows, :], waves, preferred_element_type=jnp.float32).astype(jnp.bfloat16)
-                hidden = jnp.dot(grid, w_in, preferred_element_type=jnp.float32) + b_in
-                hidden = jax.nn.gelu(hidden).astype(jnp.bfloat16)
-                value = jnp.dot(hidden, w_out, preferred_element_type=jnp.float32) + b_out
-                tend[rows, :] = value.astype(jnp.bfloat16)
-                return carry
-
-            lax.fori_loop(0, NLON // TILE, columns, 0)
+            grid = jnp.dot(tinv[...], waves, preferred_element_type=jnp.float32).astype(jnp.bfloat16)
+            hidden = jnp.dot(grid, w_in, preferred_element_type=jnp.float32) + b_in
+            hidden = jax.nn.gelu(hidden).astype(jnp.bfloat16)
+            value = jnp.dot(hidden, w_out, preferred_element_type=jnp.float32) + b_out
+            tend[...] = value.astype(jnp.bfloat16)
             coeffs = jnp.dot(tfwd[...], tend[...], preferred_element_type=jnp.float32)
             bsend[h] = coeffs.reshape(PN, KP, 128).astype(jnp.bfloat16)
 
-            def return_plane(k, carry):
-                other = (me + k) % PN
+            for step in PLANE_FAR_FIRST:
+                other = plane_other(me, step)
                 pltpu.make_async_remote_copy(
                     bsend.at[h, other], brecv.at[h, me], bs_sem.at[h], br_sem.at[h],
                     device_id=device(other, z), device_id_type=MESH,
                 ).start()
-                return carry
-
-            lax.fori_loop(1, PN, return_plane, 0)
             pltpu.make_async_copy(bsend.at[h, me], brecv.at[h, me], br_sem.at[h]).start()
+
+        def return_z(h, low, high):
+            for step in FAR_FIRST:
+                other = (z + step) % ZN
+
+                @pl.when(jnp.logical_and(other >= low, other < high))
+                def _():
+                    pltpu.make_async_remote_copy(
+                        zbsend.at[h, other], zbrecv.at[h, slot], zbs_sem.at[h], zbr_sem.at[h],
+                        device_id=device(me, other), device_id_type=MESH,
+                    ).start()
 
         for h in range(2):
             pltpu.make_async_copy(brecv.at[h], brecv.at[h], br_sem.at[h]).wait()
@@ -242,21 +255,26 @@
                         [t[g * 8 : g * 8 + 8] for t in turned], axis=0
                     ).astype(jnp.bfloat16)
 
-            def return_z(k, carry):
-                other = (z + far_first(k)) % ZN
-                pltpu.make_async_remote_copy(
-                    zbsend.at[h, other], zbrecv.at[h, slot], zbs_sem.at[h], zbr_sem.at[h],
-                    device_id=device(me, other), device_id_type=MESH,
-                ).start()
-                return carry
-
-            lax.fori_loop(1, ZN, return_z, 0)
+            for chunk, low, high in RETURN_ORDER[h]:
+                return_z(chunk, low, high)
             pltpu.make_async_copy(zbsend.at[h, z], zbrecv.at[h, slot], zbr_sem.at[h]).start()
 
     for h in range(2):
         pltpu.make_async_copy(zbrecv.at[h], zbrecv.at[h], zbr_sem.at[h]).wait()
 
-    weight_load.wait()
+    wait_z(1)
+
+    @pl.when(active)
+    def _():
+        for h in range(2):
+            pltpu.make_async_copy(psend.at[h, 0:31], psend.at[h, 0:31], ps_sem.at[h]).wait()
+            pltpu.make_async_copy(bsend.at[h, 0:31], bsend.at[h, 0:31], bs_sem.at[h]).wait()
+            pltpu.make_async_copy(zbsend.at[h, 0:15], zbsend.at[h, 0:15], zbs_sem.at[h]).wait()
+
+
+def last_sums(zbrecv, leg, qw_ref, out_ref, spec32):
+    even_lane = lax.broadcasted_iota(jnp.int32, (1, WAVES), 1) % 2 == 0
+
     weight = qw_ref[...].reshape(1, WAVES)
     got = [[zbrecv[h, s].astype(jnp.float32) for s in range(SLOTS)] for h in range(2)]
     for m in range(OWN_M):
@@ -284,32 +302,18 @@
         for b, width in enumerate((128, 128, 64)):
             out_ref[i, :, 128 * b : 128 * b + width] = spec32[b, 2 * i : 2 * i + 2, 0:width]
 
-    @pl.when(active)
-    def _():
-        for h in range(2):
-            pltpu.make_async_copy(zsend.at[h, 0:9], zsend.at[h, 0:9], zs_sem.at[h]).wait()
-            pltpu.make_async_copy(psend.at[h, 0:31], psend.at[h, 0:31], ps_sem.at[h]).wait()
-            pltpu.make_async_copy(bsend.at[h, 0:31], bsend.at[h, 0:31], bs_sem.at[h]).wait()
-            pltpu.make_async_copy(zbsend.at[h, 0:15], zbsend.at[h, 0:15], zbs_sem.at[h]).wait()
-
-    @pl.when(jnp.logical_not(active))
-    def _():
-        for h in range(2):
-            pltpu.make_async_copy(zsend.at[h], zsend.at[h], zs_sem.at[h]).wait()
-
 
 def shards(tinv, tfwd, spectral, legendre, quad_weight, w_in, b_in, w_out, b_out):
     bf16, f32 = jnp.bfloat16, jnp.float32
     vmem, hbm = (pl.BlockSpec(memory_space=s) for s in (pltpu.VMEM, pltpu.HBM))
-    out = pl.pallas_call(
+    back = pl.pallas_call(
         kernel,
-        out_shape=jax.ShapeDtypeStruct((16 * OWN_M, 2, WAVES), f32),
-        in_specs=[hbm] * 9,
+        out_shape=jax.ShapeDtypeStruct((2, SLOTS, 8 * OWN_M, 128), bf16),
+        in_specs=[hbm] * 8,
         out_specs=vmem,
         scratch_shapes=[
             pltpu.VMEM((16 * OWN_M, 2, WAVES), bf16),
             pltpu.VMEM(legendre.shape, bf16),
-            pltpu.VMEM(quad_weight.shape, f32),
             pltpu.VMEM(w_in.shape, bf16),
             pltpu.VMEM((1, w_in.shape[1]), f32),
             pltpu.VMEM(w_out.shape, bf16),
@@ -326,16 +330,24 @@
             pltpu.VMEM((2, PN, KP, 128), bf16),
             pltpu.VMEM((2, PN, KP, 128), bf16),
             pltpu.VMEM((2, ZN, 8 * OWN_M, 128), bf16),
-            pltpu.VMEM((2, SLOTS, 8 * OWN_M, 128), bf16),
-            pltpu.SemaphoreType.DMA((9,)),
+            pltpu.SemaphoreType.DMA((8,)),
         ]
         + [pltpu.SemaphoreType.DMA((2,))] * 8,
         compiler_params=pltpu.CompilerParams(collective_id=0, has_side_effects=True, vmem_limit_bytes=56 << 20),
         name="transform_step",
     )(
-        spectral.transpose(0, 1, 3, 2, 4).reshape(16 * OWN_M, 2, WAVES), legendre, quad_weight,
+        spectral.transpose(0, 1, 3, 2, 4).reshape(16 * OWN_M, 2, WAVES), legendre,
         w_in, b_in.reshape(1, -1), w_out, b_out.reshape(1, -1), tinv, tfwd,
     )
+    out = pl.pallas_call(
+        last_sums,
+        out_shape=jax.ShapeDtypeStruct((16 * OWN_M, 2, WAVES), f32),
+        in_specs=[vmem] * 3,
+        out_specs=vmem,
+        scratch_shapes=[pltpu.VMEM((3, 32 * OWN_M, 128), f32)],
+        compiler_params=pltpu.CompilerParams(vmem_limit_bytes=56 << 20),
+        name="last_sums",
+    )(back, legendre, quad_weight)
     return out.reshape(8, 2, OWN_M, 2, WAVES).transpose(0, 1, 3, 2, 4)
 
 

time: 61.2 us -> 58.5 us (0.956)
  local copies, waits for them, and re-layouts: 1.69 us -> 0 us
  Pallas kernels: 59.3 us -> 58.3 us
    unnamed x1 -> x0, local copies, waits for them, and re-layouts: 1.69 us -> none
    pallas_call x1 -> x2, Pallas kernels: 59.3 us -> 58.3 us  [the longest x1 55.7 us: shards(): pl.pallas_call(kernel, out_shape=jax.ShapeDtypeStruct((2, SLOTS, 8 * OWN_...]
where the time goes in v3:
time: 58.5 us; the launch traced here: 58.3 us
  Pallas kernels  58.3 us (100%)
    pallas_call x1, Pallas kernels, shards(): pl.pallas_call(kernel, out_shape=jax.ShapeDtypeStruct((2, SLOTS, 8 * OWN_...  55.7 us
    pallas_call x1, Pallas kernels, shards(): pl.pallas_call(last_sums, out_shape=jax.ShapeDtypeStruct((16 * OWN_M, 2,...  2.59 us

profile of v3, /device:TPU:1, one launch (start us, length us, event | category | flops | bytes accessed | tf_op | source)
XLA Modules:
  0.0 58.3 jit_solution(9018999580024123112)
XLA Ops:
  0.0 55.7 %transform_step.1.zbrecv = bf16[2,10,40,128]{3,2,1,0:T(8,128)(2,1)} custom-call(bf16[80,2,320]{2,1,0:T(2,128)(2,1)} %bitcast.8, bf16[5,320,320]{2,1,0:T(8,128)(2,1)} %leg.1, bf16[128,256]{1,0:T(8,128)(2,1)} %w_in_hbm.1, f32[1,256]{1,0:T(1,128)} %bitcast.9, bf16[256,128]{1,0:T(8,128)(2,1)} %w_out_hbm.1, f32[1,128]{1,0:T(1,128)} %bitcast.10, ...), custom_call_target="tpu_custom_call" | custom-call | tf_op jit(solution)/shard_map/transform_step/pallas_call | solution.py:309
  55.7 2.6 %last_sums.1 = f32[80,2,320]{2,1,0:T(2,128)} custom-call(bf16[2,10,40,128]{3,2,1,0:T(8,128)(2,1)} %transform_step.1.zbrecv, bf16[5,320,320]{2,1,0:T(8,128)(2,1)} %leg.1, f32[320]{0:T(512)} %qw_ref.1), custom_call_target="tpu_custom_call" | custom-call | tf_op jit(solution)/shard_map/last_sums/pallas_call | solution.py:342

commit v4 on v3

--- a/solution.py
+++ b/solution.py
@@ -149,20 +149,24 @@
         def _():
             pltpu.make_async_copy(zsend.at[h], zsend.at[h], zs_sem.at[h]).wait()
 
-    for h in range(2):
+    def send_z(h, low, high, inside):
         for k in FAR_FIRST:
             other = (z + k) % ZN
             other_slot, other_active = slot_of(other)
-
-            @pl.when(other_active)
+            within = jnp.logical_and(other >= low, other < high)
+            within = within if inside else jnp.logical_not(within)
+
+            @pl.when(jnp.logical_and(other_active, within))
             def _():
                 pltpu.make_async_remote_copy(
                     zsend.at[h, other_slot], zrecv.at[h, z], zs_sem.at[h], zr_sem.at[h],
                     device_id=device(me, other), device_id_type=MESH,
                 ).start()
 
-        if h == 0:
-            wait_z(0)
+    send_z(0, 0, ZN, True)
+    wait_z(0)
+    send_z(1, 5, 12, True)
+    send_z(1, 5, 12, False)
 
     @pl.when(active)
     def _():
@@ -345,7 +349,7 @@
         in_specs=[vmem] * 3,
         out_specs=vmem,
         scratch_shapes=[pltpu.VMEM((3, 32 * OWN_M, 128), f32)],
-        compiler_params=pltpu.CompilerParams(vmem_limit_bytes=56 << 20),
+        compiler_params=pltpu.CompilerParams(vmem_limit_bytes=8 << 20),
         name="last_sums",
     )(back, legendre, quad_weight)
     return out.reshape(8, 2, OWN_M, 2, WAVES).transpose(0, 1, 3, 2, 4)

time: 58.5 us -> 57.6 us (0.985)
  Pallas kernels: 58.3 us -> 56.5 us
  local copies, waits for them, and re-layouts: 0 us -> 0.93 us
    pallas_call x1, Pallas kernels: 2.59 us -> 1.29 us  [shards(): pl.pallas_call(last_sums, out_shape=jax.ShapeDtypeStruct((16 * OWN_M, 2,...]
    unnamed x0 -> x6, local copies, waits for them, and re-layouts: none -> 0.93 us
where the time goes in v4:
time: 57.6 us; the launch traced here: 57.5 us
  Pallas kernels  56.5 us (98%)
  local copies, waits for them, and re-layouts  0.93 us (2%)
    pallas_call x1, Pallas kernels, shards(): pl.pallas_call(kernel, out_shape=jax.ShapeDtypeStruct((2, SLOTS, 8 * OWN_...  55.2 us
    pallas_call x1, Pallas kernels, shards(): pl.pallas_call(last_sums, out_shape=jax.ShapeDtypeStruct((16 * OWN_M, 2,...  1.29 us

profile of v4, /device:TPU:1, one launch (start us, length us, event | category | flops | bytes accessed | tf_op | source)
XLA Modules:
  0.0 57.5 jit_solution(17772097257216769327)
XLA Ops:
  0.0 0.0 copy-start
  0.0 0.0 copy-start.2
  0.0 55.2 %transform_step.1.zbrecv = bf16[2,10,40,128]{3,2,1,0:T(8,128)(2,1)} custom-call(bf16[80,2,320]{2,1,0:T(2,128)(2,1)} %bitcast.8, bf16[5,320,320]{2,1,0:T(8,128)(2,1)} %leg.1, bf16[128,256]{1,0:T(8,128)(2,1)} %w_in_hbm.1, f32[1,256]{1,0:T(1,128)} %bitcast.9, bf16[256,128]{1,0:T(8,128)(2,1)} %w_out_hbm.1, f32[1,128]{1,0:T(1,128)} %bitcast.10, ...), custom_call_target="tpu_custom_call" | custom-call | tf_op jit(solution)/shard_map/transform_step/pallas_call | solution.py:313
  55.2 0.0 copy-done
  55.2 0.0 copy-done.2
  55.3 0.0 copy-start.1
  55.3 0.9 %copy-done.1 = bf16[2,10,40,128]{3,2,1,0:T(8,128)(2,1)S(1)} copy-done((bf16[2,10,40,128]{3,2,1,0:T(8,128)(2,1)S(1)}, bf16[2,10,40,128]{3,2,1,0:T(8,128)(2,1)}, u32[]{:S(2)}) %copy-start.1) | copy-done | bytes 204824
  56.2 1.3 %last_sums.1 = f32[80,2,320]{2,1,0:T(2,128)} custom-call(bf16[2,10,40,128]{3,2,1,0:T(8,128)(2,1)S(1)} %copy-done.1, bf16[5,320,320]{2,1,0:T(8,128)(2,1)S(1)} %copy-done, f32[320]{0:T(512)S(1)} %copy-done.2), custom_call_target="tpu_custom_call" | custom-call | tf_op jit(solution)/shard_map/last_sums/pallas_call | solution.py:346
Async XLA Ops:
  0.0 55.2 %copy-start = (bf16[5,320,320]{2,1,0:T(8,128)(2,1)S(1)}, bf16[5,320,320]{2,1,0:T(8,128)(2,1)}, u32[]{:S(2)}) copy-start(bf16[5,320,320]{2,1,0:T(8,128)(2,1)} %leg.1) | copy-start | bytes 3072004
  0.0 55.2 %copy-start.2 = (f32[320]{0:T(512)S(1)}, f32[320]{0:T(512)}, u32[]{:S(2)}) copy-start(f32[320]{0:T(512)} %qw_ref.1) | copy-start | bytes 3844
  55.3 0.9 %copy-start.1 = (bf16[2,10,40,128]{3,2,1,0:T(8,128)(2,1)S(1)}, bf16[2,10,40,128]{3,2,1,0:T(8,128)(2,1)}, u32[]{:S(2)}) copy-start(bf16[2,10,40,128]{3,2,1,0:T(8,128)(2,1)} %transform_step.1.zbrecv) | copy-start | bytes 614404

commit v5 on v4

--- a/solution.py
+++ b/solution.py
@@ -48,7 +48,7 @@
 
 
 FAR_FIRST = (8, 7, 9, 6, 10, 5, 11, 4, 12, 3, 13, 2, 14, 1, 15)
-RETURN_ORDER = (((0, 0, 6),), ((1, 0, 3), (1, 3, 6), (0, 6, 16), (1, 6, 16)))
+RETURN_ORDER = (((0, 0, 10),), ((1, 0, 3), (1, 3, 6), (0, 10, 16), (1, 6, 16)))
 
 
 def away(step):

time: 57.6 us -> 56.8 us (0.986)
  Pallas kernels: 56.5 us -> 55.7 us
    pallas_call x1, Pallas kernels: 55.2 us -> 54.4 us  [shards(): pl.pallas_call(kernel, out_shape=jax.ShapeDtypeStruct((2, SLOTS, 8 * OWN_...]
where the time goes in v5:
time: 56.8 us; the launch traced here: 56.7 us
  Pallas kernels  55.7 us (98%)
  local copies, waits for them, and re-layouts  0.93 us (2%)
    pallas_call x1, Pallas kernels, shards(): pl.pallas_call(kernel, out_shape=jax.ShapeDtypeStruct((2, SLOTS, 8 * OWN_...  54.4 us
    pallas_call x1, Pallas kernels, shards(): pl.pallas_call(last_sums, out_shape=jax.ShapeDtypeStruct((16 * OWN_M, 2,...  1.29 us

profile of v5, /device:TPU:1, one launch (start us, length us, event | category | flops | bytes accessed | tf_op | source)
XLA Modules:
  0.0 56.7 jit_solution(9287244090090982266)
XLA Ops:
  0.0 0.0 copy-start
  0.0 0.0 copy-start.2
  0.0 54.4 %transform_step.1.zbrecv = bf16[2,10,40,128]{3,2,1,0:T(8,128)(2,1)} custom-call(bf16[80,2,320]{2,1,0:T(2,128)(2,1)} %bitcast.8, bf16[5,320,320]{2,1,0:T(8,128)(2,1)} %leg.1, bf16[128,256]{1,0:T(8,128)(2,1)} %w_in_hbm.1, f32[1,256]{1,0:T(1,128)} %bitcast.9, bf16[256,128]{1,0:T(8,128)(2,1)} %w_out_hbm.1, f32[1,128]{1,0:T(1,128)} %bitcast.10, ...), custom_call_target="tpu_custom_call" | custom-call | tf_op jit(solution)/shard_map/transform_step/pallas_call | solution.py:313
  54.5 0.0 copy-done
  54.5 0.0 copy-done.2
  54.5 0.0 copy-start.1
  54.5 0.9 %copy-done.1 = bf16[2,10,40,128]{3,2,1,0:T(8,128)(2,1)S(1)} copy-done((bf16[2,10,40,128]{3,2,1,0:T(8,128)(2,1)S(1)}, bf16[2,10,40,128]{3,2,1,0:T(8,128)(2,1)}, u32[]{:S(2)}) %copy-start.1) | copy-done | bytes 204824
  55.4 1.3 %last_sums.1 = f32[80,2,320]{2,1,0:T(2,128)} custom-call(bf16[2,10,40,128]{3,2,1,0:T(8,128)(2,1)S(1)} %copy-done.1, bf16[5,320,320]{2,1,0:T(8,128)(2,1)S(1)} %copy-done, f32[320]{0:T(512)S(1)} %copy-done.2), custom_call_target="tpu_custom_call" | custom-call | tf_op jit(solution)/shard_map/last_sums/pallas_call | solution.py:346
Async XLA Ops:
  0.0 54.5 %copy-start = (bf16[5,320,320]{2,1,0:T(8,128)(2,1)S(1)}, bf16[5,320,320]{2,1,0:T(8,128)(2,1)}, u32[]{:S(2)}) copy-start(bf16[5,320,320]{2,1,0:T(8,128)(2,1)} %leg.1) | copy-start | bytes 3072004
  0.0 54.5 %copy-start.2 = (f32[320]{0:T(512)S(1)}, f32[320]{0:T(512)}, u32[]{:S(2)}) copy-start(f32[320]{0:T(512)} %qw_ref.1) | copy-start | bytes 3844
  54.5 0.9 %copy-start.1 = (bf16[2,10,40,128]{3,2,1,0:T(8,128)(2,1)S(1)}, bf16[2,10,40,128]{3,2,1,0:T(8,128)(2,1)}, u32[]{:S(2)}) copy-start(bf16[2,10,40,128]{3,2,1,0:T(8,128)(2,1)} %transform_step.1.zbrecv) | copy-start | bytes 614404

commit v6 on v5

--- a/solution.py
+++ b/solution.py
@@ -233,10 +233,9 @@
             pltpu.make_async_copy(bsend.at[h, me], brecv.at[h, me], br_sem.at[h]).start()
 
         def return_z(h, low, high):
-            for step in FAR_FIRST:
-                other = (z + step) % ZN
-
-                @pl.when(jnp.logical_and(other >= low, other < high))
+            for other in range(low, high):
+
+                @pl.when(other != z)
                 def _():
                     pltpu.make_async_remote_copy(
                         zbsend.at[h, other], zbrecv.at[h, slot], zbs_sem.at[h], zbr_sem.at[h],

time: 56.8 us -> 56.5 us (level); the launches traced: 56.7 us -> 55.7 us
  Pallas kernels: 55.7 us -> 54.7 us
    pallas_call x1, Pallas kernels: 54.4 us -> 53.5 us  [shards(): pl.pallas_call(kernel, out_shape=jax.ShapeDtypeStruct((2, SLOTS, 8 * OWN_...]
where the time goes in v6:
time: 56.5 us; the launch traced here: 55.7 us
  Pallas kernels  54.7 us (97%)
  local copies, waits for them, and re-layouts  0.93 us (2%)
    pallas_call x1, Pallas kernels, shards(): pl.pallas_call(kernel, out_shape=jax.ShapeDtypeStruct((2, SLOTS, 8 * OWN_...  53.5 us
    pallas_call x1, Pallas kernels, shards(): pl.pallas_call(last_sums, out_shape=jax.ShapeDtypeStruct((16 * OWN_M, 2,...  1.29 us

profile of v6, /device:TPU:1, one launch (start us, length us, event | category | flops | bytes accessed | tf_op | source)
XLA Modules:
  0.0 55.7 jit_solution(73501924210824411)
XLA Ops:
  0.0 0.0 copy-start
  0.0 0.0 copy-start.2
  0.0 53.5 %transform_step.1.zbrecv = bf16[2,10,40,128]{3,2,1,0:T(8,128)(2,1)} custom-call(bf16[80,2,320]{2,1,0:T(2,128)(2,1)} %bitcast.8, bf16[5,320,320]{2,1,0:T(8,128)(2,1)} %leg.1, bf16[128,256]{1,0:T(8,128)(2,1)} %w_in_hbm.1, f32[1,256]{1,0:T(1,128)} %bitcast.9, bf16[256,128]{1,0:T(8,128)(2,1)} %w_out_hbm.1, f32[1,128]{1,0:T(1,128)} %bitcast.10, ...), custom_call_target="tpu_custom_call" | custom-call | tf_op jit(solution)/shard_map/transform_step/pallas_call | solution.py:312
  53.5 0.0 copy-done
  53.5 0.0 copy-done.2
  53.5 0.0 copy-start.1
  53.5 0.9 %copy-done.1 = bf16[2,10,40,128]{3,2,1,0:T(8,128)(2,1)S(1)} copy-done((bf16[2,10,40,128]{3,2,1,0:T(8,128)(2,1)S(1)}, bf16[2,10,40,128]{3,2,1,0:T(8,128)(2,1)}, u32[]{:S(2)}) %copy-start.1) | copy-done | bytes 204824
  54.4 1.3 %last_sums.1 = f32[80,2,320]{2,1,0:T(2,128)} custom-call(bf16[2,10,40,128]{3,2,1,0:T(8,128)(2,1)S(1)} %copy-done.1, bf16[5,320,320]{2,1,0:T(8,128)(2,1)S(1)} %copy-done, f32[320]{0:T(512)S(1)} %copy-done.2), custom_call_target="tpu_custom_call" | custom-call | tf_op jit(solution)/shard_map/last_sums/pallas_call | solution.py:345
Async XLA Ops:
  0.0 53.5 %copy-start = (bf16[5,320,320]{2,1,0:T(8,128)(2,1)S(1)}, bf16[5,320,320]{2,1,0:T(8,128)(2,1)}, u32[]{:S(2)}) copy-start(bf16[5,320,320]{2,1,0:T(8,128)(2,1)} %leg.1) | copy-start | bytes 3072004
  0.0 53.5 %copy-start.2 = (f32[320]{0:T(512)S(1)}, f32[320]{0:T(512)}, u32[]{:S(2)}) copy-start(f32[320]{0:T(512)} %qw_ref.1) | copy-start | bytes 3844
  53.5 0.9 %copy-start.1 = (bf16[2,10,40,128]{3,2,1,0:T(8,128)(2,1)S(1)}, bf16[2,10,40,128]{3,2,1,0:T(8,128)(2,1)}, u32[]{:S(2)}) copy-start(bf16[2,10,40,128]{3,2,1,0:T(8,128)(2,1)} %transform_step.1.zbrecv) | copy-start | bytes 614404
